TPU v7x, 32 devices: a whole 2x2x4 slice. The times are simulated.
32 devices in a mesh: gx: 4 (over z), gy: 8 (over y, x, core).
Axes of the slice: x: 2, y: 2, z: 4, core: 2. Of those that a mesh axis runs over, the one named last changes fastest.
Arguments:
- embeddings: bfloat16 [393216, 256], P(('gx', 'gy'))
- start: float32 [32, 393216], P(None, ('gx', 'gy'))
- requests: int32 [32, 8], P(('gx', 'gy')), may hold values from -1 to 23, as said below
- pairs: int32 [32, 40, 2], P(('gx', 'gy')), may hold values from 0 to 31, as said below
- counts: int32 [32], P(('gx', 'gy')), may hold values from 24 to 40, as said below
Outputs:
- spectral: float32 [32, 393216], P(None, ('gx', 'gy'))
Inputs may be any that keep to these rules, and one draw needn't show every extreme that they name: requests[d, q] is -1 where q is d's own index along gy; every entry that is not -1 is used by some live slot of d. A live slot (a, s) has a < 24; if s < 24 then a <= s, else requests[d, s - 24] >= 0; every block of a device has a live slot (a, a); local pairs of one device are distinct; slots at or beyond counts[d] are (0, 0). counts[d] = 24 + (entries of requests[d] that are not -1) + (slots pairing two different blocks of d); in every gx group some device has all 40 slots live.
All inputs are finite; a program needn't handle non-finite values.
Results may differ from a plain program's by a relative error of at most 0.0046.
Values may be sent and summed in bfloat16 or wider, within the bound.
A program may use at most 192 MiB of HBM per device.

v0:
```python
import jax
import jax.numpy as jnp
from jax import lax
from jax.sharding import PartitionSpec as P

D = 256
VECS = 32
BLK = 512
ITERS = 2


tiles_per_turn = 8


def normalize(raw_rows):
    values = raw_rows.astype(jnp.float32)
    scaled = values * lax.rsqrt(jnp.sum(values * values, axis=-1, keepdims=True) + 1e-06)
    return scaled.astype(jnp.bfloat16)


def to_blocks(matrix, block_count):
    return matrix.reshape(matrix.shape[0], block_count, BLK).transpose(1, 0, 2)


def columns(slot_index, near_src, far_src):
    block_count = near_src.shape[0]
    inside = slot_index < block_count
    own_pick = near_src[jnp.clip(slot_index, 0, block_count - 1)]
    far_pick = far_src[jnp.clip(slot_index - block_count, 0, far_src.shape[0] - 1)]
    return jnp.where(inside[:, None, None], own_pick, far_pick)


def per_device(embeddings, start, requests, pairs, counts):
    peer_count = lax.axis_size("gy")
    row_total = embeddings.shape[0]
    block_count = row_total // BLK
    rows_all = row_total * lax.axis_size("gx") * peer_count
    unit_blocks = normalize(embeddings).reshape(block_count, BLK, D)
    wanted = lax.all_to_all(
        requests.reshape(peer_count, 1), "gy", split_axis=0, concat_axis=0, tiled=True
    )[:, 0]
    served = wanted >= 0
    served_weight = served.astype(jnp.float32)
    wanted_block = jnp.maximum(wanted, 0)

    def outgoing(source):
        picked = source[wanted_block]
        return jnp.where(served[:, None, None], picked, jnp.zeros_like(picked))

    near_vecs = to_blocks(start.astype(jnp.bfloat16), block_count)
    far_vecs = None
    far_rows = lax.all_to_all(outgoing(unit_blocks), "gy", split_axis=0, concat_axis=0, tiled=True)
    slot_total = pairs.shape[1]
    padded = -(-slot_total // tiles_per_turn) * tiles_per_turn
    row_slot = pairs[0, :, 0]
    col_slot = pairs[0, :, 1]
    live_count = counts[0]
    slot_live = jnp.arange(padded, dtype=jnp.int32) < live_count
    turn_count = (live_count + tiles_per_turn - 1) // tiles_per_turn
    row_slot = jnp.clip(row_slot, 0, block_count - 1)
    live_weight = slot_live.astype(jnp.float32)
    both_weight = (slot_live & (row_slot != col_slot)).astype(jnp.float32)

    def build_group(turn_id, tile_stack):
        offset = turn_id * tiles_per_turn
        row_part = lax.dynamic_slice_in_dim(row_slot, offset, tiles_per_turn)
        col_part = lax.dynamic_slice_in_dim(col_slot, offset, tiles_per_turn)
        left_rows = unit_blocks[row_part]
        right_rows = columns(col_part, unit_blocks, far_rows)
        product = jnp.einsum(
            "grd,gcd->grc", left_rows, right_rows, preferred_element_type=jnp.float32
        )
        return lax.dynamic_update_slice_in_dim(
            tile_stack, (product * product * product).astype(jnp.bfloat16), offset, 0
        )

    tile_stack = lax.fori_loop(
        0, turn_count, build_group, jnp.zeros((padded, BLK, BLK), jnp.bfloat16)
    )
    vectors = start
    for iteration in range(ITERS):
        if iteration > 0:
            near_vecs = to_blocks(vectors.astype(jnp.bfloat16), block_count)
        far_vecs = lax.all_to_all(
            outgoing(near_vecs), "gy", split_axis=0, concat_axis=0, tiled=True
        )
        partial_value = jnp.zeros((block_count + peer_count, VECS, BLK), jnp.float32)
        near_src = near_vecs
        far_src = far_vecs

        def add_group(turn_id, running):
            offset = turn_id * tiles_per_turn
            row_part = lax.dynamic_slice_in_dim(row_slot, offset, tiles_per_turn)
            col_part = lax.dynamic_slice_in_dim(col_slot, offset, tiles_per_turn)
            live_part = lax.dynamic_slice_in_dim(live_weight, offset, tiles_per_turn)
            both_part = lax.dynamic_slice_in_dim(both_weight, offset, tiles_per_turn)
            tile_group = lax.dynamic_slice_in_dim(tile_stack, offset, tiles_per_turn)
            row_vecs = near_src[row_part]
            col_vecs = columns(col_part, near_src, far_src)
            to_row = (
                jnp.einsum("gkc,grc->gkr", col_vecs, tile_group, preferred_element_type=jnp.float32)
                * live_part[:, None, None]
            )
            to_col = (
                jnp.einsum("gkr,grc->gkc", row_vecs, tile_group, preferred_element_type=jnp.float32)
                * both_part[:, None, None]
            )
            return running.at[row_part].add(to_row).at[col_part].add(to_col)

        partial_value = lax.fori_loop(0, turn_count, add_group, partial_value)
        returned = lax.all_to_all(
            partial_value[block_count:], "gy", split_axis=0, concat_axis=0, tiled=True
        )
        own_rows = (
            partial_value[:block_count]
            .at[wanted_block]
            .add(returned * served_weight[:, None, None])
        )
        flat_rows = own_rows.transpose(1, 0, 2).reshape(VECS, row_total)
        local_gram = jnp.dot(
            flat_rows,
            flat_rows.T,
            precision=lax.Precision.HIGHEST,
            preferred_element_type=jnp.float32,
        )
        gram_matrix = lax.psum(local_gram, ("gx", "gy"))
        lower_factor = jnp.linalg.cholesky(gram_matrix / rows_all)
        vectors = lax.linalg.triangular_solve(lower_factor, flat_rows, left_side=True, lower=True)
    return vectors


def solution(mesh):
    return jax.shard_map(
        per_device,
        mesh=mesh,
        in_specs=(
            P(("gx", "gy"), None),
            P(None, ("gx", "gy")),
            P(("gx", "gy"), None),
            P(("gx", "gy"), None, None),
            P(("gx", "gy")),
        ),
        out_specs=P(None, ("gx", "gy")),
        check_vma=False,
    )
```

profile of v0, /device:TPU:0, one launch (start us, length us, event | category | flops | bytes accessed | tf_op | source)
XLA Modules:
  0.0 430.8 jit_solution(12125808189232617065)
XLA Ops:
  1.3 5.2 %all-to-all-start = ((s32[8,1,1]{2,1,0:T(1,128)}), s32[8,1,1]{2,1,0:T(1,128)S(1)}, u32[]{:S(2)}, u32[]{:S(2)}) async-start(s32[8,1,1]{2,1,0:T(1,128)} %copy.39), calls=%async_computation | async-start | bytes 8192 | tf_op jit(solution)/shard_map/all_to_all | solution.py:39
  6.5 4.8 %fusion.32 = f32[12288]{0:T(1024)S(1)} fusion(bf16[12288,256]{1,0:T(8,128)(2,1)} %param.14), kind=kLoop, calls=%fused_computation.71 | loop fusion | flops 9424896 | bytes 6340608 | tf_op jit(solution)/shard_map/reduce_sum | solution.py:17
  11.4 4.0 fusion.33
  20.9 4.2 all-to-all-start.2
  28.8 22.9 %all-to-all-done.2 = bf16[8,512,256]{2,1,0:T(8,128)(2,1)S(1)} async-done(((bf16[8,512,256]{2,1,0:T(8,128)(2,1)}), bf16[8,512,256]{2,1,0:T(8,128)(2,1)S(1)}, u32[]{:S(2)}, u32[]{:S(2)}) %all-to-all-start.2) | async-done | bytes 2097184 | tf_op jit(solution)/shard_map/all_to_all | solution.py:52
  55.1 7.1 %broadcast_in_dim.156 = bf16[40,512,512]{2,1,0:T(8,128)(2,1)} broadcast(bf16[]{:T(256)} %constant.197.clone.1), dimensions={} | broadcast | bytes 20971522 | tf_op jit(solution)/shard_map/broadcast_in_dim | solution.py:78
  62.3 71.7 %while.36 = (s32[]{:T(128)}, bf16[40,512,512]{2,1,0:T(8,128)(2,1)}, s32[]{:T(128)}, s32[40]{0:T(128)S(1)}, bf16[24,512,256]{2,1,0:T(8,128)(2,1)}, /*index=5*/s32...) while((s32[]{:T(128)}, bf16[40,512,512]{2,1,0:T(8,128)(2,1)}, ...), condition=%wide.region_2.3_spmd, body=%wide.region_1.2_spmd.sunk | while | flops 1081085056 | bytes 23081528 | solution.py:77
  62.4 4.8 %gather_fusion = bf16[8,512,256]{2,1,0:T(8,128)(2,1)} fusion(bf16[24,512,256]{2,1,0:T(8,128)(2,1)} %get-tuple-element.679, s32[1024]{0:T(1024)S(1)} %pad_clamp_fusion.19), kind=kCustom, calls=%fused_computation.clone.1 | custom fusion | bytes 4194336 | tf_op jit(solution)/shard_map/while/body/gather | solution.py:68
  67.1 4.8 %gather_fusion.1 = bf16[8,512,256]{2,1,0:T(8,128)(2,1)} fusion(bf16[24,512,256]{2,1,0:T(8,128)(2,1)} %get-tuple-element.679, s32[1024]{0:T(1024)S(1)} %pad_clamp_fusion.20), kind=kCustom, calls=%fused_computation.1.clone.1 | custom fusion | bytes 4194336 | tf_op jit(solution)/shard_map/while/body/gather | solution.py:28
  74.0 6.2 %fusion.75 = bf16[40,512,512]{2,1,0:T(8,128)(2,1)} fusion(bf16[40,512,512]{2,1,0:T(8,128)(2,1)} %get-tuple-element.665, s32[]{:T(128)S(6)} %select_n.198, bf16[8,512,256]{2,1,0:T(8,128)(2,1)} %gather_fusion, bf16[8,512,256]{2,1,0:T(8,128)(2,1)} %gather_fusion.1, bf16[8,512,256]{2,1,0:T(8,128)(2,1)} %gather_fusion.2, ...), kind=kOutput, calls=%fused_computation.20.clone.1 | convolution fusion | flops 1081081856 | bytes 10485772 | tf_op jit(solution)/shard_map/while/body/grd,gcd->grc/dot_general | solution.py:70
  80.3 4.8 %gather_fusion = bf16[8,512,256]{2,1,0:T(8,128)(2,1)} fusion(bf16[24,512,256]{2,1,0:T(8,128)(2,1)} %get-tuple-element.679, s32[1024]{0:T(1024)S(1)} %pad_clamp_fusion.19), kind=kCustom, calls=%fused_computation.clone.1 | custom fusion | bytes 4194336 | tf_op jit(solution)/shard_map/while/body/gather | solution.py:68
  85.0 4.8 %gather_fusion.1 = bf16[8,512,256]{2,1,0:T(8,128)(2,1)} fusion(bf16[24,512,256]{2,1,0:T(8,128)(2,1)} %get-tuple-element.679, s32[1024]{0:T(1024)S(1)} %pad_clamp_fusion.20), kind=kCustom, calls=%fused_computation.1.clone.1 | custom fusion | bytes 4194336 | tf_op jit(solution)/shard_map/while/body/gather | solution.py:28
  91.9 6.2 %fusion.75 = bf16[40,512,512]{2,1,0:T(8,128)(2,1)} fusion(bf16[40,512,512]{2,1,0:T(8,128)(2,1)} %get-tuple-element.665, s32[]{:T(128)S(6)} %select_n.198, bf16[8,512,256]{2,1,0:T(8,128)(2,1)} %gather_fusion, bf16[8,512,256]{2,1,0:T(8,128)(2,1)} %gather_fusion.1, bf16[8,512,256]{2,1,0:T(8,128)(2,1)} %gather_fusion.2, ...), kind=kOutput, calls=%fused_computation.20.clone.1 | convolution fusion | flops 1081081856 | bytes 10485772 | tf_op jit(solution)/shard_map/while/body/grd,gcd->grc/dot_general | solution.py:70
  98.2 4.8 %gather_fusion = bf16[8,512,256]{2,1,0:T(8,128)(2,1)} fusion(bf16[24,512,256]{2,1,0:T(8,128)(2,1)} %get-tuple-element.679, s32[1024]{0:T(1024)S(1)} %pad_clamp_fusion.19), kind=kCustom, calls=%fused_computation.clone.1 | custom fusion | bytes 4194336 | tf_op jit(solution)/shard_map/while/body/gather | solution.py:68
  103.0 4.8 %gather_fusion.1 = bf16[8,512,256]{2,1,0:T(8,128)(2,1)} fusion(bf16[24,512,256]{2,1,0:T(8,128)(2,1)} %get-tuple-element.679, s32[1024]{0:T(1024)S(1)} %pad_clamp_fusion.20), kind=kCustom, calls=%fused_computation.1.clone.1 | custom fusion | bytes 4194336 | tf_op jit(solution)/shard_map/while/body/gather | solution.py:28
  109.9 6.2 %fusion.75 = bf16[40,512,512]{2,1,0:T(8,128)(2,1)} fusion(bf16[40,512,512]{2,1,0:T(8,128)(2,1)} %get-tuple-element.665, s32[]{:T(128)S(6)} %select_n.198, bf16[8,512,256]{2,1,0:T(8,128)(2,1)} %gather_fusion, bf16[8,512,256]{2,1,0:T(8,128)(2,1)} %gather_fusion.1, bf16[8,512,256]{2,1,0:T(8,128)(2,1)} %gather_fusion.2, ...), kind=kOutput, calls=%fused_computation.20.clone.1 | convolution fusion | flops 1081081856 | bytes 10485772 | tf_op jit(solution)/shard_map/while/body/grd,gcd->grc/dot_general | solution.py:70
  116.2 4.8 %gather_fusion = bf16[8,512,256]{2,1,0:T(8,128)(2,1)} fusion(bf16[24,512,256]{2,1,0:T(8,128)(2,1)} %get-tuple-element.679, s32[1024]{0:T(1024)S(1)} %pad_clamp_fusion.19), kind=kCustom, calls=%fused_computation.clone.1 | custom fusion | bytes 4194336 | tf_op jit(solution)/shard_map/while/body/gather | solution.py:68
  120.9 4.8 %gather_fusion.1 = bf16[8,512,256]{2,1,0:T(8,128)(2,1)} fusion(bf16[24,512,256]{2,1,0:T(8,128)(2,1)} %get-tuple-element.679, s32[1024]{0:T(1024)S(1)} %pad_clamp_fusion.20), kind=kCustom, calls=%fused_computation.1.clone.1 | custom fusion | bytes 4194336 | tf_op jit(solution)/shard_map/while/body/gather | solution.py:28
  127.8 6.2 %fusion.75 = bf16[40,512,512]{2,1,0:T(8,128)(2,1)} fusion(bf16[40,512,512]{2,1,0:T(8,128)(2,1)} %get-tuple-element.665, s32[]{:T(128)S(6)} %select_n.198, bf16[8,512,256]{2,1,0:T(8,128)(2,1)} %gather_fusion, bf16[8,512,256]{2,1,0:T(8,128)(2,1)} %gather_fusion.1, bf16[8,512,256]{2,1,0:T(8,128)(2,1)} %gather_fusion.2, ...), kind=kOutput, calls=%fused_computation.20.clone.1 | convolution fusion | flops 1081081856 | bytes 10485772 | tf_op jit(solution)/shard_map/while/body/grd,gcd->grc/dot_general | solution.py:70
  134.3 51.5 %while.37 = (s32[]{:T(128)}, f32[32,32,512]{2,1,0:T(8,128)S(1)}, s32[]{:T(128)}, s32[40]{0:T(128)S(1)}, s32[40]{0:T(128)S(1)}, /*index=5*/bf16[24,32,512]{2,1,0:...) while((s32[]{:T(128)}, f32[32,32,512]{2,1,0:T(8,128)S(1)}, ...), condition=%wide.region_6.7_spmd, body=%wide.region_3.6_spmd.sunk | while | flops 269094016 | bytes 14955479 | solution.py:110
  136.8 3.5 fusion.80
  149.7 3.5 fusion.80
  162.5 3.5 fusion.80
  186.6 34.0 %all-to-all-start.3 = ((f32[8,32,512]{2,1,0:T(8,128)}), f32[8,32,512]{2,1,0:T(8,128)S(1)}, u32[]{:S(2)}, u32[]{:S(2)}) async-start(f32[8,32,512]{2,1,0:T(8,128)} %slice.27), calls=%async_computation.3 | async-start | bytes 1048576 | tf_op jit(solution)/shard_map/all_to_all | solution.py:111
  221.9 8.4 %all-to-all-done.3 = f32[8,32,512]{2,1,0:T(8,128)S(1)} async-done(((f32[8,32,512]{2,1,0:T(8,128)}), f32[8,32,512]{2,1,0:T(8,128)S(1)}, u32[]{:S(2)}, u32[]{:S(2)}) %all-to-all-start.3) | async-done | bytes 524320 | tf_op jit(solution)/shard_map/all_to_all | solution.py:111
  236.6 40.8 %psum.14 = f32[32,32]{0,1:T(8,128)S(1)} all-reduce(f32[32,32]{0,1:T(8,128)S(1)} %fusion.38), channel_id=1, replica_groups=mesh['gx'=4,'gy'=8] {'gx','gy'}, use_global_device_ids=true, to_apply=%region_8.9 | all-reduce | flops 1024 | bytes 8192 | tf_op jit(solution)/shard_map/psum | solution.py:126
  287.2 3.6 all-to-all-start.4
  290.8 6.9 %all-to-all-done.4 = bf16[8,32,512]{2,1,0:T(8,128)(2,1)S(1)} async-done(((bf16[8,32,512]{2,1,0:T(8,128)(2,1)}), bf16[8,32,512]{2,1,0:T(8,128)(2,1)S(1)}, u32[]{:S(2)}, u32[]{:S(2)}) %all-to-all-start.4) | async-done | bytes 262176 | tf_op jit(solution)/shard_map/all_to_all | solution.py:84
  298.0 51.4 %while.38 = (s32[]{:T(128)}, f32[32,32,512]{2,1,0:T(8,128)S(1)}, s32[]{:T(128)}, s32[40]{0:T(128)S(1)}, s32[40]{0:T(128)S(1)}, /*index=5*/bf16[24,32,512]{2,1,0:...) while((s32[]{:T(128)}, f32[32,32,512]{2,1,0:T(8,128)S(1)}, ...), condition=%wide.region_14.17_spmd, body=%wide.region_11.16_spmd.sunk | while | flops 269094016 | bytes 14955479 | solution.py:110
  350.3 14.7 %all-to-all-start.5 = ((f32[8,32,512]{2,1,0:T(8,128)}), f32[8,32,512]{2,1,0:T(8,128)S(1)}, u32[]{:S(2)}, u32[]{:S(2)}) async-start(f32[8,32,512]{2,1,0:T(8,128)} %slice.29), calls=%async_computation.5 | async-start | bytes 1048576 | tf_op jit(solution)/shard_map/all_to_all | solution.py:111
  366.3 8.4 %all-to-all-done.5 = f32[8,32,512]{2,1,0:T(8,128)S(1)} async-done(((f32[8,32,512]{2,1,0:T(8,128)}), f32[8,32,512]{2,1,0:T(8,128)S(1)}, u32[]{:S(2)}, u32[]{:S(2)}) %all-to-all-start.5) | async-done | bytes 524320 | tf_op jit(solution)/shard_map/all_to_all | solution.py:111
  381.0 40.1 %psum.15 = f32[32,32]{0,1:T(8,128)S(1)} all-reduce(f32[32,32]{0,1:T(8,128)S(1)} %fusion.41), channel_id=1, replica_groups=mesh['gx'=4,'gy'=8] {'gx','gy'}, use_global_device_ids=true, to_apply=%region_16.19 | all-reduce | flops 1024 | bytes 8192 | tf_op jit(solution)/shard_map/psum | solution.py:126
  (205 shorter events, 150.3 us)
Async XLA Ops:
  1.3 14.0 %all-to-all-start = ((s32[8,1,1]{2,1,0:T(1,128)}), s32[8,1,1]{2,1,0:T(1,128)S(1)}, u32[]{:S(2)}, u32[]{:S(2)}) async-start(s32[8,1,1]{2,1,0:T(1,128)} %copy.39), calls=%async_computation | async-start | bytes 8192 | tf_op jit(solution)/shard_map/all_to_all | solution.py:39
  6.5 4.9 %copy-start = (bf16[12288,256]{1,0:T(8,128)(2,1)S(1)}, bf16[12288,256]{1,0:T(8,128)(2,1)}, u32[]{:S(2)}) copy-start(bf16[12288,256]{1,0:T(8,128)(2,1)} %param.14) | copy-start | bytes 18874372
  20.9 30.8 %all-to-all-start.2 = ((bf16[8,512,256]{2,1,0:T(8,128)(2,1)}), bf16[8,512,256]{2,1,0:T(8,128)(2,1)S(1)}, u32[]{:S(2)}, u32[]{:S(2)}) async-start(bf16[8,512,256]{2,1,0:T(8,128)(2,1)} %broadcast_select_fusion), calls=%async_computation.2 | async-start | bytes 4194304 | tf_op jit(solution)/shard_map/all_to_all | solution.py:52
  25.1 2.3 copy-start.5
  27.3 34.9 %copy-start.3 = (bf16[4,24,8,512]{3,2,0,1:T(8,128)(2,1)}, bf16[4,24,8,512]{3,2,0,1:T(8,128)(2,1)S(1)}, u32[]{:S(2)}) copy-start(bf16[4,24,8,512]{3,2,0,1:T(8,128)(2,1)S(1)} %copy.58) | copy-start | bytes 2359300
  51.7 82.3 %all-to-all-start.1 = ((bf16[8,32,512]{2,1,0:T(8,128)(2,1)}), bf16[8,32,512]{2,1,0:T(8,128)(2,1)S(1)}, u32[]{:S(2)}, u32[]{:S(2)}) async-start(bf16[8,32,512]{2,1,0:T(8,128)(2,1)} %broadcast_select_fusion.2), calls=%async_computation.1 | async-start | bytes 524288 | tf_op jit(solution)/shard_map/all_to_all | solution.py:84
  186.6 43.7 %all-to-all-start.3 = ((f32[8,32,512]{2,1,0:T(8,128)}), f32[8,32,512]{2,1,0:T(8,128)S(1)}, u32[]{:S(2)}, u32[]{:S(2)}) async-start(f32[8,32,512]{2,1,0:T(8,128)} %slice.27), calls=%async_computation.3 | async-start | bytes 1048576 | tf_op jit(solution)/shard_map/all_to_all | solution.py:111
  233.1 51.0 %copy-start.2 = (f32[24,32,512]{2,1,0:T(8,128)S(1)}, f32[24,32,512]{2,1,0:T(8,128)}, u32[]{:S(2)}) copy-start(f32[24,32,512]{2,1,0:T(8,128)} %scatter_fusion.4) | copy-start | bytes 4718596
  285.9 4.9 %copy-start.4 = (bf16[4,24,8,512]{3,2,0,1:T(8,128)(2,1)}, bf16[4,24,8,512]{3,2,0,1:T(8,128)(2,1)S(1)}, u32[]{:S(2)}) copy-start(bf16[4,24,8,512]{3,2,0,1:T(8,128)(2,1)S(1)} %copy.57) | copy-start | bytes 2359300
  287.2 10.5 %all-to-all-start.4 = ((bf16[8,32,512]{2,1,0:T(8,128)(2,1)}), bf16[8,32,512]{2,1,0:T(8,128)(2,1)S(1)}, u32[]{:S(2)}, u32[]{:S(2)}) async-start(bf16[8,32,512]{2,1,0:T(8,128)(2,1)} %broadcast_select_fusion.1), calls=%async_computation.4 | async-start | bytes 524288 | tf_op jit(solution)/shard_map/all_to_all | solution.py:84
  350.3 24.4 %all-to-all-start.5 = ((f32[8,32,512]{2,1,0:T(8,128)}), f32[8,32,512]{2,1,0:T(8,128)S(1)}, u32[]{:S(2)}, u32[]{:S(2)}) async-start(f32[8,32,512]{2,1,0:T(8,128)} %slice.29), calls=%async_computation.5 | async-start | bytes 1048576 | tf_op jit(solution)/shard_map/all_to_all | solution.py:111
  377.5 50.5 %copy-start.1 = (f32[24,32,512]{2,1,0:T(8,128)S(1)}, f32[24,32,512]{2,1,0:T(8,128)}, u32[]{:S(2)}) copy-start(f32[24,32,512]{2,1,0:T(8,128)} %scatter_fusion.5) | copy-start | bytes 4718596
where the time goes:
time: 434 us; the launch traced here: 431 us
  local copies, waits for them, and re-layouts  97.8 us (23%)
  matrix products  87.2 us (20%)
  blocking collectives  80.9 us (19%)
  starting transfers between devices  65 us (15%)
  other arithmetic  51.3 us (12%)
  waiting for transfers between devices  46.8 us (11%)
    psum x2, blocking collectives, per_device(): gram_matrix = lax.psum(local_gram, ('gx', 'gy'))  80.9 us
    all_to_all x2, starting transfers between devices, per_device(): lax.all_to_all(partial_value[block_count:], 'gy', split_axis=0, concat_ax...  48.7 us
    gather x12, local copies, waits for them, and re-layouts, columns(): own_pick = near_src[jnp.clip(slot_index, 0, block_count - 1)]  32.9 us
    dot_general x8, matrix products, add_group(): jnp.einsum('gkc,grc->gkr', col_vecs, tile_group, preferred_element_type=j...  28 us
    dot_general x4, matrix products, build_group(): jnp.einsum('grd,gcd->grc', left_rows, right_rows, preferred_element_type=...  24.7 us
    dot_general x8, matrix products, add_group(): jnp.einsum('gkr,grc->gkc', row_vecs, tile_group, preferred_element_type=j...  23.4 us
    all_to_all x1, waiting for transfers between devices, per_device(): lax.all_to_all(outgoing(unit_blocks), 'gy', split_axis=0, concat_axis=0,...  22.9 us
    gather x4, local copies, waits for them, and re-layouts, build_group(): left_rows = unit_blocks[row_part]  19 us
  transfers between devices with their start and end apart: 6, of which 4 were waited for; matrix products, arithmetic and copies ran while one was open for 22% of the time, Pallas kernels for 0%

commit v1 on v0

v1 whole, which is shorter than its diff:
```python
import functools

import jax
import jax.numpy as jnp
from jax import lax
from jax.experimental import pallas as pl
from jax.experimental.pallas import tpu as pltpu
from jax.sharding import PartitionSpec as P

D = 256
VECS = 32
BLK = 512
ITERS = 2
HALF = 256
MESH = pl.DeviceIdType.MESH
F32 = jnp.float32
BF16 = jnp.bfloat16


def normalize(raw_rows):
    values = raw_rows.astype(F32)
    scaled = values * lax.rsqrt(jnp.sum(values * values, axis=-1, keepdims=True) + 1e-06)
    return scaled.astype(BF16)


def dot_nn(a, b):
    return lax.dot_general(a, b, (((1,), (0,)), ((), ())), preferred_element_type=F32)


def dot_nt(a, b):
    return lax.dot_general(a, b, (((1,), (1,)), ((), ())), preferred_element_type=F32)


def split3(x):
    high = x.astype(BF16)
    rest = x - high.astype(F32)
    mid = rest.astype(BF16)
    low = (rest - mid.astype(F32)).astype(BF16)
    return jnp.concatenate([high, mid, low], axis=0)


def inverse_factor(gram):
    row = lax.broadcasted_iota(jnp.int32, (VECS, 4 * VECS), 0)
    lane = lax.broadcasted_iota(jnp.int32, (VECS, 4 * VECS), 1)
    eye = ((lane % VECS) == row).astype(F32)
    work = jnp.concatenate([eye[:, : 3 * VECS], gram], axis=1)
    for k in range(VECS):
        pivot_row = work[k : k + 1, :]
        column = work[:, 3 * VECS + k : 3 * VECS + k + 1]
        pivot = work[k : k + 1, 3 * VECS + k : 3 * VECS + k + 1]
        factor = jnp.where(row[:, :1] > k, column / pivot, 0.0)
        work = work - factor * pivot_row
    pivots = jnp.sum(jnp.where(lane == row + 3 * VECS, work, 0.0), axis=1, keepdims=True)
    return work[:, : 3 * VECS] * lax.rsqrt(pivots)


def kernel(
    peers, groups, extra, stash, rows_all,
    table, req, emb, start, out,
    req_all, wanted, unit, near_w, tiles, image, split,
    rows_send, rows_far, w_send, w_far, ex_row, ex_col, far_row, ret_send, ret_far,
    gram_y, gram_x,
    local_sem, req_s, req_r, rows_s, rows_r, w_s, w_r, ret_s, ret_r, gy_s, gy_r, gx_s, gx_r,
):
    blocks = emb.shape[0]
    gx = lax.axis_index("gx")
    me = lax.axis_index("gy")

    def ahead(o):
        return lax.rem(me + o, peers)

    def behind(o):
        return lax.rem(me + peers - o, peers)

    def remote(src, dst, s_sem, r_sem, target):
        return pltpu.make_async_remote_copy(
            src_ref=src, dst_ref=dst, send_sem=s_sem, recv_sem=r_sem,
            device_id=target, device_id_type=MESH,
        )

    def req_copy(o):
        return remote(req, req_all.at[o - 1], req_s.at[o - 1], req_r.at[o - 1], (gx, ahead(o)))

    def rows_copy(o):
        return remote(
            rows_send.at[o - 1], rows_far.at[o - 1], rows_s.at[o - 1], rows_r.at[o - 1],
            (gx, behind(o)),
        )

    def w_copy(it, o):
        return remote(
            w_send.at[it, o - 1], w_far.at[it, o - 1], w_s.at[it, o - 1], w_r.at[it, o - 1],
            (gx, behind(o)),
        )

    def ret_copy(it, o):
        return remote(
            ret_send.at[it, o - 1], ret_far.at[it, o - 1], ret_s.at[it, o - 1],
            ret_r.at[it, o - 1], (gx, ahead(o)),
        )

    def gy_copy(it, o):
        return remote(
            gram_y.at[it, me], gram_y.at[it, me], gy_s.at[it, o - 1], gy_r.at[it, o - 1],
            (gx, ahead(o)),
        )

    def gx_copy(it, o):
        return remote(
            gram_x.at[it, gx], gram_x.at[it, gx], gx_s.at[it, o - 1], gx_r.at[it, o - 1],
            (lax.rem(gx + o, groups), me),
        )

    def each(count, body, first=0, unroll=1):
        def step(i, carry):
            body(i)
            return carry

        lax.fori_loop(first, count, step, 0, unroll=unroll)

    def block_columns(b):
        return pl.ds(pl.multiple_of(b * BLK, BLK), BLK)

    barrier = pltpu.get_barrier_semaphore()
    each(
        peers,
        lambda o: pl.semaphore_signal(barrier, inc=1, device_id=(gx, ahead(o)), device_id_type=MESH),
        1,
    )
    each(
        groups,
        lambda o: pl.semaphore_signal(
            barrier, inc=1, device_id=(lax.rem(gx + o, groups), me), device_id_type=MESH
        ),
        1,
    )
    pl.semaphore_wait(barrier, peers + groups - 2)

    each(peers, lambda o: req_copy(o).start(), 1)

    def round_start(b):
        near_w[b] = start[:, block_columns(b)].astype(BF16)

    each(blocks, round_start, unroll=2)

    each(peers, lambda o: req_copy(o).wait(), 1)
    to_scalar = pltpu.make_async_copy(req_all, wanted, local_sem)
    to_scalar.start()
    to_scalar.wait()

    def send_w(it):
        def body(o):
            index = jnp.maximum(wanted[o - 1, 0, me], 0)
            w_send[it, o - 1] = near_w[index]
            w_copy(it, o).start()

        each(peers, body, 1)

    send_w(0)

    def send_rows(o):
        index = jnp.maximum(wanted[o - 1, 0, me], 0)
        rows_send[o - 1] = normalize(emb[index])
        rows_copy(o).start()

    each(peers, send_rows, 1)

    def build(slot, left, right):
        for part in range(BLK // HALF):
            span = pl.ds(part * HALF, HALF)
            product = dot_nt(left[part * HALF : (part + 1) * HALF], right)
            tiles[slot, span, :] = (product * product * product).astype(BF16)

    for it in range(ITERS):
        fresh = it == 0 or not stash

        def diagonal(b):
            slot = b if stash else 0
            if it == 0:
                unit[b] = normalize(emb[b])
            if fresh:
                rows = unit[b]
                build(slot, rows, rows)
            image[b] = dot_nn(near_w[b], tiles[slot])

        each(blocks, diagonal, unroll=2)

        def local_pair(e):
            slot = blocks + e if stash else 0
            left = jnp.maximum(table[peers + e], 0)
            right = jnp.maximum(table[peers + extra + e], 0)
            if fresh:
                build(slot, unit[left], unit[right])
            ex_row[e] = dot_nt(near_w[right], tiles[slot])
            ex_col[e] = dot_nn(near_w[left], tiles[slot])

        each(extra, local_pair)

        def add_local(b):
            total = image[b]
            for e in range(extra):
                total += (table[peers + e] == b).astype(F32) * ex_row[e]
                total += (table[peers + extra + e] == b).astype(F32) * ex_col[e]
            image[b] = total

        each(blocks, add_local)

        def far_pair(o):
            slot = blocks + extra + o - 1 if stash else 0
            left = jnp.maximum(table[ahead(o)], 0)
            if it == 0:
                rows_copy(o).wait_recv()
            w_copy(it, o).wait_recv()
            if fresh:
                build(slot, unit[left], rows_far[o - 1])
            ret_send[it, o - 1] = dot_nn(near_w[left], tiles[slot])
            ret_copy(it, o).start()
            far_row[o - 1] = dot_nt(w_far[it, o - 1], tiles[slot])

        each(peers, far_pair, 1)

        def add_far(b):
            total = image[b]
            for o in range(1, peers):
                total += (table[ahead(o)] == b).astype(F32) * far_row[o - 1]
            image[b] = total

        each(blocks, add_far)

        each(peers, lambda o: ret_copy(it, o).wait_recv(), 1)

        def add_returned(b):
            total = image[b]
            for o in range(1, peers):
                total += (wanted[o - 1, 0, me] == b).astype(F32) * ret_far[it, o - 1]
            split[:, block_columns(b)] = split3(total)

        each(blocks, add_returned)

        parts = split[...]
        products = dot_nt(parts, parts)
        products = products[:VECS] + products[VECS : 2 * VECS] + products[2 * VECS :]
        gram = products[:, :VECS] + products[:, VECS : 2 * VECS] + products[:, 2 * VECS :]
        gram_y[it, me] = jnp.concatenate([gram[8 * i : 8 * i + 8] for i in range(4)], axis=1)
        each(peers, lambda o: gy_copy(it, o).start(), 1)

        def gy_wait(o):
            remote(
                gram_y.at[it, me], gram_y.at[it, behind(o)], gy_s.at[it, o - 1],
                gy_r.at[it, o - 1], (gx, ahead(o)),
            ).wait_recv()

        each(peers, gy_wait, 1)
        each(peers, lambda o: gy_copy(it, o).wait_send(), 1)
        gram_x[it, gx] = jnp.sum(gram_y[it], axis=0)
        each(groups, lambda o: gx_copy(it, o).start(), 1)

        def gx_wait(o):
            remote(
                gram_x.at[it, gx], gram_x.at[it, lax.rem(gx + groups - o, groups)],
                gx_s.at[it, o - 1], gx_r.at[it, o - 1], (lax.rem(gx + o, groups), me),
            ).wait_recv()

        each(groups, gx_wait, 1)
        each(groups, lambda o: gx_copy(it, o).wait_send(), 1)
        packed = jnp.sum(gram_x[it], axis=0)
        gram = jnp.concatenate(
            [packed[:, VECS * i : VECS * (i + 1)] for i in range(4)], axis=0
        )
        factor = split3(inverse_factor(gram / rows_all))

        def apply_factor(b):
            triple = dot_nn(factor, split[:, block_columns(b)])
            result = triple[:VECS] + triple[VECS : 2 * VECS] + triple[2 * VECS :]
            if it < ITERS - 1:
                near_w[b] = result.astype(BF16)
            else:
                out[:, block_columns(b)] = result

        each(blocks, apply_factor, unroll=2)
        if it < ITERS - 1:
            send_w(it + 1)

    each(peers, lambda o: req_copy_done(o, rows_copy, w_copy, ret_copy), 1)


def req_copy_done(o, rows_copy, w_copy, ret_copy):
    rows_copy(o).wait_send()
    for it in range(ITERS):
        w_copy(it, o).wait_send()
        ret_copy(it, o).wait_send()


def slot_table(pairs, counts, blocks, peers, extra):
    slots = pairs.shape[1]
    row_slot, col_slot = pairs[0, :, 0], pairs[0, :, 1]
    index = jnp.arange(slots, dtype=jnp.int32)
    live = index < counts[0]
    far = live[None, :] & (col_slot[None, :] == blocks + jnp.arange(peers, dtype=jnp.int32)[:, None])
    local = live & (col_slot < blocks) & (row_slot != col_slot)
    before = jnp.sum((local[None, :] & (index[None, :] < index[:, None])).astype(jnp.int32), axis=1)
    near = local[None, :] & (before[None, :] == jnp.arange(extra, dtype=jnp.int32)[:, None])

    def pick(mask, values):
        return jnp.sum(jnp.where(mask, values[None, :] + 1, 0), axis=1) - 1

    return jnp.concatenate([pick(far, row_slot), pick(near, row_slot), pick(near, col_slot)])


def per_device(embeddings, start, requests, pairs, counts):
    peers = lax.axis_size("gy")
    groups = lax.axis_size("gx")
    row_total = embeddings.shape[0]
    blocks = row_total // BLK
    extra = pairs.shape[1] - blocks - (peers - 1)
    stash = peers <= 8
    tile_count = blocks + extra + peers - 1 if stash else 1
    table = slot_table(pairs, counts, blocks, peers, extra)
    req = jnp.pad(requests, ((0, 7), (0, 128 - peers)), constant_values=-1)
    hops = peers - 1
    dma = pltpu.SemaphoreType.DMA
    vmem = pl.BlockSpec(memory_space=pltpu.VMEM)
    return pl.pallas_call(
        functools.partial(kernel, peers, groups, extra, stash, float(row_total * groups * peers)),
        out_shape=jax.ShapeDtypeStruct(start.shape, F32),
        in_specs=[pl.BlockSpec(memory_space=pltpu.SMEM), vmem, vmem, vmem],
        out_specs=vmem,
        scratch_shapes=[
            pltpu.VMEM((hops, 8, 128), jnp.int32),
            pltpu.SMEM((hops, 8, 128), jnp.int32),
            pltpu.VMEM((blocks, BLK, D), BF16),
            pltpu.VMEM((blocks, VECS, BLK), BF16),
            pltpu.VMEM((tile_count, BLK, BLK), BF16),
            pltpu.VMEM((blocks, VECS, BLK), F32),
            pltpu.VMEM((3 * VECS, row_total), BF16),
            pltpu.VMEM((hops, BLK, D), BF16),
            pltpu.VMEM((hops, BLK, D), BF16),
            pltpu.VMEM((ITERS, hops, VECS, BLK), BF16),
            pltpu.VMEM((ITERS, hops, VECS, BLK), BF16),
            pltpu.VMEM((extra, VECS, BLK), F32),
            pltpu.VMEM((extra, VECS, BLK), F32),
            pltpu.VMEM((hops, VECS, BLK), F32),
            pltpu.VMEM((ITERS, hops, VECS, BLK), F32),
            pltpu.VMEM((ITERS, hops, VECS, BLK), F32),
            pltpu.VMEM((ITERS, peers, 8, 128), F32),
            pltpu.VMEM((ITERS, groups, 8, 128), F32),
            dma,
            dma((hops,)),
            dma((hops,)),
            dma((hops,)),
            dma((hops,)),
            dma((ITERS, hops)),
            dma((ITERS, hops)),
            dma((ITERS, hops)),
            dma((ITERS, hops)),
            dma((ITERS, hops)),
            dma((ITERS, hops)),
            dma((ITERS, groups - 1)),
            dma((ITERS, groups - 1)),
        ],
        compiler_params=pltpu.CompilerParams(
            collective_id=0, has_side_effects=True, vmem_limit_bytes=60 * 1024 * 1024
        ),
    )(table, req, embeddings.reshape(blocks, BLK, D), start)


def solution(mesh):
    return jax.shard_map(
        per_device,
        mesh=mesh,
        in_specs=(
            P(("gx", "gy"), None),
            P(None, ("gx", "gy")),
            P(("gx", "gy"), None),
            P(("gx", "gy"), None, None),
            P(("gx", "gy")),
        ),
        out_specs=P(None, ("gx", "gy")),
        check_vma=False,
    )
```

time: 434 us -> 103 us (0.24)
  Pallas kernels: 0 us -> 94.7 us
  local copies, waits for them, and re-layouts: 97.8 us -> 4.59 us
  matrix products: 87.2 us -> 0 us
  blocking collectives: 80.9 us -> 0 us
  starting transfers between devices: 65 us -> 0 us
  other arithmetic: 51.3 us -> 2.57 us
  waiting for transfers between devices: 46.8 us -> 0 us
    pallas_call x0 -> x1, Pallas kernels: none -> 94.7 us  [per_device(): pl.pallas_call(functools.partial(kernel, peers, groups, extra, stash, flo...]
    dot_general x22 -> x0, matrix products: 83.2 us -> none  [the longest x8 28 us: add_group(): jnp.einsum('gkc,grc->gkr', col_vecs, tile_group, preferred_element_type=j...]
    gather x39 -> x0, local copies, waits for them, and re-layouts: 82.6 us -> none  [the longest x12 32.9 us: columns(): own_pick = near_src[jnp.clip(slot_index, 0, block_count - 1)]]
    psum x2 -> x0, blocking collectives: 80.9 us -> none  [per_device(): gram_matrix = lax.psum(local_gram, ('gx', 'gy'))]
    all_to_all x6 -> x0, starting transfers between devices: 65 us -> none  [the longest x2 48.7 us: per_device(): lax.all_to_all(partial_value[block_count:], 'gy', split_axis=0, concat_ax...]
    all_to_all x6 -> x0, waiting for transfers between devices: 46.8 us -> none  [the longest x1 22.9 us: per_device(): lax.all_to_all(outgoing(unit_blocks), 'gy', split_axis=0, concat_axis=0,...]
    scatter-add x18 -> x0, other arithmetic: 22.1 us -> none  [the longest x16 16.8 us: add_group(): return running.at[row_part].add(to_row).at[col_part].add(to_col)]
    another operation x10 -> x0, other arithmetic: 13.5 us -> none  [the longest x6 7.3 us: per_device(): lower_factor = jnp.linalg.cholesky(gram_matrix / rows_all)]
  transfers between devices with their start and end apart: 6 -> 0, of which waited for: 4 -> 0; matrix products, arithmetic and copies ran while one was open for 22% -> 0% of each run, Pallas kernels for 0% -> 0%
where the time goes in v1:
time: 103 us
  Pallas kernels  94.7 us (92%)
  local copies, waits for them, and re-layouts  4.59 us (4%)
  other arithmetic  2.57 us (2%)
    pallas_call x1, Pallas kernels, per_device(): pl.pallas_call(functools.partial(kernel, peers, groups, extra, stash, flo...  94.7 us
    unnamed x1, local copies, waits for them, and re-layouts  2.65 us

profile of v1, /device:TPU:0, one launch (start us, length us, event | category | flops | bytes accessed | tf_op | source)
XLA Modules:
  0.0 102.5 jit_solution(13786027233355970473)
XLA Ops:
  0.7 0.7 slice_bitcast_fusion
  1.3 0.8 compare_and_fusion
  2.1 0.1 convert_reduce_fusion
  2.2 0.8 broadcast_add_fusion.3
  3.0 0.2 select_reduce_fusion.2
  3.2 0.1 select_reduce_fusion.1
  3.3 0.6 pad_add_fusion.table
  3.9 1.3 %pad.4.req = s32[8,128]{1,0:T(8,128)} pad(s32[1,8]{1,0:T(1,128)} %param.7, s32[]{:T(128)} %constant.3.clone.1), padding=0_7x0_120 | pad | bytes 4132 | tf_op jit(solution)/shard_map/jit(_pad)/pad | solution.py:319
  5.2 94.7 %shard_map.55 = f32[32,12288]{1,0:T(8,128)} custom-call(s32[26]{0:T(128)} %pad_add_fusion.table, s32[8,128]{1,0:T(8,128)} %pad.4.req, bf16[24,512,256]{2,1,0:T(8,128)(2,1)} %bitcast.12, f32[32,12288]{1,0:T(8,128)} %start.1), custom_call_target="tpu_custom_call" | custom-call | tf_op jit(solution)/shard_map/pallas_call | solution.py:323
  99.9 2.7 %copy.8 = f32[32,12288]{1,0:T(8,128)} copy(f32[32,12288]{1,0:T(8,128)} %shard_map.55) | data formatting | bytes 3145728
  (4 shorter events, 0.0 us)

commit v2 on v1

--- a/solution.py
+++ b/solution.py
@@ -44,23 +44,33 @@
     lane = lax.broadcasted_iota(jnp.int32, (VECS, 4 * VECS), 1)
     eye = ((lane % VECS) == row).astype(F32)
     work = jnp.concatenate([eye[:, : 3 * VECS], gram], axis=1)
-    for k in range(VECS):
-        pivot_row = work[k : k + 1, :]
-        column = work[:, 3 * VECS + k : 3 * VECS + k + 1]
-        pivot = work[k : k + 1, 3 * VECS + k : 3 * VECS + k + 1]
-        factor = jnp.where(row[:, :1] > k, column / pivot, 0.0)
-        work = work - factor * pivot_row
+    shape = (VECS, 4 * VECS)
+    base = 3 * VECS
+    for k in range(0, VECS, 2):
+        first = jnp.broadcast_to(work[:, base + k : base + k + 1], shape)
+        second = jnp.broadcast_to(work[:, base + k + 1 : base + k + 2], shape)
+        row0, row1 = work[k : k + 1, :], work[k + 1 : k + 2, :]
+        scale = 1.0 / first[k : k + 1, :]
+        ratio = first[k + 1 : k + 2, :] * scale
+        below = row1 - ratio * row0
+        second = second - first * ratio
+        inverse = 1.0 / second[k + 1 : k + 2, :]
+        work = (
+            work
+            - jnp.where(row > k, first, 0.0) * (scale * row0)
+            - jnp.where(row > k + 1, second, 0.0) * (inverse * below)
+        )
     pivots = jnp.sum(jnp.where(lane == row + 3 * VECS, work, 0.0), axis=1, keepdims=True)
     return work[:, : 3 * VECS] * lax.rsqrt(pivots)
 
 
 def kernel(
     peers, groups, extra, stash, rows_all,
-    table, req, emb, start, out,
-    req_all, wanted, unit, near_w, tiles, image, split,
+    pairs, counts, requests, emb_hbm, start_hbm, image_hbm, last_factor,
+    table, emb, start, req, req_all, wanted, unit, near_w, tiles, image, split,
     rows_send, rows_far, w_send, w_far, ex_row, ex_col, far_row, ret_send, ret_far,
     gram_y, gram_x,
-    local_sem, req_s, req_r, rows_s, rows_r, w_s, w_r, ret_s, ret_r, gy_s, gy_r, gx_s, gx_r,
+    local_sem, emb_sem, start_sem, image_sem, req_s, req_r, rows_s, rows_r, w_s, w_r, ret_s, ret_r, gy_s, gy_r, gx_s, gx_r,
 ):
     blocks = emb.shape[0]
     gx = lax.axis_index("gx")
@@ -120,6 +130,13 @@
 
     def block_columns(b):
         return pl.ds(pl.multiple_of(b * BLK, BLK), BLK)
+
+    start_in = pltpu.make_async_copy(start_hbm, start, start_sem)
+    emb_in = pltpu.make_async_copy(emb_hbm, emb, emb_sem)
+    start_in.start()
+    emb_in.start()
+    req[...] = jnp.full(req.shape, -1, jnp.int32)
+    req[0:1, 0:peers] = requests[...]
 
     barrier = pltpu.get_barrier_semaphore()
     each(
@@ -138,6 +155,9 @@
 
     each(peers, lambda o: req_copy(o).start(), 1)
 
+    fill_table(table, pairs, counts, blocks, peers, extra)
+    start_in.wait()
+
     def round_start(b):
         near_w[b] = start[:, block_columns(b)].astype(BF16)
 
@@ -157,6 +177,7 @@
         each(peers, body, 1)
 
     send_w(0)
+    emb_in.wait()
 
     def send_rows(o):
         index = jnp.maximum(wanted[o - 1, 0, me], 0)
@@ -194,16 +215,8 @@
             ex_row[e] = dot_nt(near_w[right], tiles[slot])
             ex_col[e] = dot_nn(near_w[left], tiles[slot])
 
-        each(extra, local_pair)
-
-        def add_local(b):
-            total = image[b]
-            for e in range(extra):
-                total += (table[peers + e] == b).astype(F32) * ex_row[e]
-                total += (table[peers + extra + e] == b).astype(F32) * ex_col[e]
-            image[b] = total
-
-        each(blocks, add_local)
+        if it == 0:
+            each(extra, local_pair)
 
         def far_pair(o):
             slot = blocks + extra + o - 1 if stash else 0
@@ -219,13 +232,19 @@
 
         each(peers, far_pair, 1)
 
-        def add_far(b):
+        if it > 0:
+            each(extra, local_pair)
+
+        def add_own(b):
             total = image[b]
+            for e in range(extra):
+                total += (table[peers + e] == b).astype(F32) * ex_row[e]
+                total += (table[peers + extra + e] == b).astype(F32) * ex_col[e]
             for o in range(1, peers):
                 total += (table[ahead(o)] == b).astype(F32) * far_row[o - 1]
             image[b] = total
 
-        each(blocks, add_far)
+        each(blocks, add_own)
 
         each(peers, lambda o: ret_copy(it, o).wait_recv(), 1)
 
@@ -234,9 +253,13 @@
             for o in range(1, peers):
                 total += (wanted[o - 1, 0, me] == b).astype(F32) * ret_far[it, o - 1]
             split[:, block_columns(b)] = split3(total)
+            if it == ITERS - 1:
+                image[b] = total
 
         each(blocks, add_returned)
 
+        if it == ITERS - 1:
+            pltpu.make_async_copy(image, image_hbm, image_sem).start()
         parts = split[...]
         products = dot_nt(parts, parts)
         products = products[:VECS] + products[VECS : 2 * VECS] + products[2 * VECS :]
@@ -251,7 +274,6 @@
             ).wait_recv()
 
         each(peers, gy_wait, 1)
-        each(peers, lambda o: gy_copy(it, o).wait_send(), 1)
         gram_x[it, gx] = jnp.sum(gram_y[it], axis=0)
         each(groups, lambda o: gx_copy(it, o).start(), 1)
 
@@ -262,49 +284,68 @@
             ).wait_recv()
 
         each(groups, gx_wait, 1)
-        each(groups, lambda o: gx_copy(it, o).wait_send(), 1)
         packed = jnp.sum(gram_x[it], axis=0)
         gram = jnp.concatenate(
             [packed[:, VECS * i : VECS * (i + 1)] for i in range(4)], axis=0
         )
         factor = split3(inverse_factor(gram / rows_all))
 
-        def apply_factor(b):
-            triple = dot_nn(factor, split[:, block_columns(b)])
-            result = triple[:VECS] + triple[VECS : 2 * VECS] + triple[2 * VECS :]
-            if it < ITERS - 1:
-                near_w[b] = result.astype(BF16)
-            else:
-                out[:, block_columns(b)] = result
-
-        each(blocks, apply_factor, unroll=2)
-        if it < ITERS - 1:
+        if it == ITERS - 1:
+            last_factor[...] = factor
+        else:
+
+            def apply_factor(b):
+                near_w[b] = apply_split(factor, split[:, block_columns(b)]).astype(BF16)
+
+            each(blocks, apply_factor, unroll=2)
             send_w(it + 1)
 
-    each(peers, lambda o: req_copy_done(o, rows_copy, w_copy, ret_copy), 1)
-
-
-def req_copy_done(o, rows_copy, w_copy, ret_copy):
-    rows_copy(o).wait_send()
-    for it in range(ITERS):
-        w_copy(it, o).wait_send()
-        ret_copy(it, o).wait_send()
-
-
-def slot_table(pairs, counts, blocks, peers, extra):
-    slots = pairs.shape[1]
-    row_slot, col_slot = pairs[0, :, 0], pairs[0, :, 1]
-    index = jnp.arange(slots, dtype=jnp.int32)
-    live = index < counts[0]
-    far = live[None, :] & (col_slot[None, :] == blocks + jnp.arange(peers, dtype=jnp.int32)[:, None])
-    local = live & (col_slot < blocks) & (row_slot != col_slot)
-    before = jnp.sum((local[None, :] & (index[None, :] < index[:, None])).astype(jnp.int32), axis=1)
-    near = local[None, :] & (before[None, :] == jnp.arange(extra, dtype=jnp.int32)[:, None])
-
-    def pick(mask, values):
-        return jnp.sum(jnp.where(mask, values[None, :] + 1, 0), axis=1) - 1
-
-    return jnp.concatenate([pick(far, row_slot), pick(near, row_slot), pick(near, col_slot)])
+    def finish(o):
+        rows_copy(o).wait_send()
+        for it in range(ITERS):
+            w_copy(it, o).wait_send()
+            ret_copy(it, o).wait_send()
+            gy_copy(it, o).wait_send()
+
+    def finish_x(o):
+        for it in range(ITERS):
+            gx_copy(it, o).wait_send()
+
+    each(peers, finish, 1)
+    each(groups, finish_x, 1)
+    pltpu.make_async_copy(image, image_hbm, image_sem).wait()
+
+
+def apply_split(factor, parts):
+    triple = dot_nn(factor, parts)
+    return triple[:VECS] + triple[VECS : 2 * VECS] + triple[2 * VECS :]
+
+
+def last_kernel(factor, image, out):
+    for b in range(image.shape[0]):
+        out[:, b * BLK : (b + 1) * BLK] = apply_split(factor[...], split3(image[b]))
+
+
+def fill_table(table, pairs, counts, blocks, peers, extra):
+    live_count = counts[0]
+
+    def step(k, carry):
+        seen, far, rows, cols = carry
+        r, s = pairs[0, 0, k], pairs[0, 1, k]
+        s = jnp.where(k < live_count, s, -1)
+        local = (s >= 0) & (s < blocks) & (r != s)
+        place = jnp.where(local, seen, -1)
+        far = tuple(jnp.where(s == blocks + q, r, far[q]) for q in range(peers))
+        rows = tuple(jnp.where(place == e, r, rows[e]) for e in range(extra))
+        cols = tuple(jnp.where(place == e, s, cols[e]) for e in range(extra))
+        return seen + local.astype(jnp.int32), far, rows, cols
+
+    none = jnp.int32(-1)
+    _, far, rows, cols = lax.fori_loop(
+        0, pairs.shape[2], step, (jnp.int32(0), (none,) * peers, (none,) * extra, (none,) * extra)
+    )
+    for index, value in enumerate(far + rows + cols):
+        table[index] = value
 
 
 def per_device(embeddings, start, requests, pairs, counts):
@@ -315,17 +356,24 @@
     extra = pairs.shape[1] - blocks - (peers - 1)
     stash = peers <= 8
     tile_count = blocks + extra + peers - 1 if stash else 1
-    table = slot_table(pairs, counts, blocks, peers, extra)
-    req = jnp.pad(requests, ((0, 7), (0, 128 - peers)), constant_values=-1)
     hops = peers - 1
     dma = pltpu.SemaphoreType.DMA
     vmem = pl.BlockSpec(memory_space=pltpu.VMEM)
-    return pl.pallas_call(
+    smem = pl.BlockSpec(memory_space=pltpu.SMEM)
+    hbm = pl.BlockSpec(memory_space=pl.ANY)
+    image, factor = pl.pallas_call(
         functools.partial(kernel, peers, groups, extra, stash, float(row_total * groups * peers)),
-        out_shape=jax.ShapeDtypeStruct(start.shape, F32),
-        in_specs=[pl.BlockSpec(memory_space=pltpu.SMEM), vmem, vmem, vmem],
-        out_specs=vmem,
+        out_shape=(
+            jax.ShapeDtypeStruct((blocks, VECS, BLK), F32),
+            jax.ShapeDtypeStruct((3 * VECS, 3 * VECS), BF16),
+        ),
+        in_specs=[smem, smem, vmem, hbm, hbm],
+        out_specs=(hbm, vmem),
         scratch_shapes=[
+            pltpu.SMEM((peers + 2 * extra,), jnp.int32),
+            pltpu.VMEM((blocks, BLK, D), BF16),
+            pltpu.VMEM(start.shape, F32),
+            pltpu.VMEM((8, 128), jnp.int32),
             pltpu.VMEM((hops, 8, 128), jnp.int32),
             pltpu.SMEM((hops, 8, 128), jnp.int32),
             pltpu.VMEM((blocks, BLK, D), BF16),
@@ -345,6 +393,9 @@
             pltpu.VMEM((ITERS, peers, 8, 128), F32),
             pltpu.VMEM((ITERS, groups, 8, 128), F32),
             dma,
+            dma,
+            dma,
+            dma,
             dma((hops,)),
             dma((hops,)),
             dma((hops,)),
@@ -361,7 +412,19 @@
         compiler_params=pltpu.CompilerParams(
             collective_id=0, has_side_effects=True, vmem_limit_bytes=60 * 1024 * 1024
         ),
-    )(table, req, embeddings.reshape(blocks, BLK, D), start)
+    )(pairs.swapaxes(1, 2), counts, requests, embeddings.reshape(blocks, BLK, D), start)
+    turn = next(n for n in (6, 4, 3, 2, 1) if blocks % n == 0)
+    return pl.pallas_call(
+        last_kernel,
+        out_shape=jax.ShapeDtypeStruct(start.shape, F32),
+        grid=(blocks // turn,),
+        in_specs=[
+            pl.BlockSpec((3 * VECS, 3 * VECS), lambda i: (0, 0)),
+            pl.BlockSpec((turn, VECS, BLK), lambda i: (i, 0, 0)),
+        ],
+        out_specs=pl.BlockSpec((VECS, turn * BLK), lambda i: (0, i)),
+        compiler_params=pltpu.CompilerParams(vmem_limit_bytes=60 * 1024 * 1024),
+    )(factor, image)
 
 
 def solution(mesh):

time: 103 us -> 87.6 us (0.85)
  Pallas kernels: 94.7 us -> 86.8 us
  local copies, waits for them, and re-layouts: 4.59 us -> 0 us
  other arithmetic: 2.57 us -> 0 us
    pallas_call x1, Pallas kernels: 94.7 us -> 82.6 us  [per_device(): pl.pallas_call(functools.partial(kernel, peers, groups, extra, stash, flo...]
    pallas_call x0 -> x1, Pallas kernels: none -> 4.14 us  [per_device(): pl.pallas_call(last_kernel, out_shape=jax.ShapeDtypeStruct(start.shape, F...]
    unnamed x1 -> x0, local copies, waits for them, and re-layouts: 2.65 us -> none
    pad x1 -> x0, local copies, waits for them, and re-layouts: 1.25 us -> none  [per_device(): req = jnp.pad(requests, ((0, 7), (0, 128 - peers)), constant_values=-1)]
where the time goes in v2:
time: 87.6 us; the launch traced here: 87.4 us
  Pallas kernels  86.8 us (99%)
    pallas_call x1, Pallas kernels, per_device(): pl.pallas_call(functools.partial(kernel, peers, groups, extra, stash, flo...  82.6 us
    pallas_call x1, Pallas kernels, per_device(): pl.pallas_call(last_kernel, out_shape=jax.ShapeDtypeStruct(start.shape, F...  4.14 us

profile of v2, /device:TPU:0, one launch (start us, length us, event | category | flops | bytes accessed | tf_op | source)
XLA Modules:
  0.0 87.4 jit_solution(8702700088592157318)
XLA Ops:
  0.7 82.6 %shard_map.55 = (f32[24,32,512]{2,1,0:T(8,128)}, bf16[96,96]{1,0:T(8,128)(2,1)}) custom-call(s32[1,2,40]{2,1,0:T(2,128)} %bitcast.3, s32[1]{0:T(128)S(6)} %copy.6.counts, s32[1,8]{1,0:T(1,128)} %requests.1, bf16[24,512,256]{2,1,0:T(8,128)(2,1)} %bitcast.2, f32[32,12288]{1,0:T(8,128)} %start_hbm.1), custom_call_target="tpu_custom_call" | custom-call | tf_op jit(solution)/shard_map/pallas_call | solution.py:364
  83.3 4.1 %shard_map.56 = f32[32,12288]{1,0:T(8,128)} custom-call(bf16[96,96]{1,0:T(8,128)(2,1)} %get-tuple-element.7.factor, f32[24,32,512]{2,1,0:T(8,128)} %get-tuple-element.8.image), custom_call_target="tpu_custom_call" | custom-call | tf_op jit(solution)/shard_map/pallas_call | solution.py:417
